TPU v7x, 32 devices: a whole 2x2x4 slice. The times are simulated.
32 devices in a mesh: groups: 2 (over y), rows: 4 (over z), tiles: 2 (over x), sub: 2 (over core).
Axes of the slice: x: 2, y: 2, z: 4, core: 2. Of those that a mesh axis runs over, the one named last changes fastest.
Arguments:
- points: float32 [20480, 64], P(('groups', 'rows')), parts along dimension 0, may hold values from -6 to 6
- targets: float32 [20480, 128], P(('groups', 'rows', 'tiles', 'sub')), parts along dimension 0, may hold values from -6 to 6
- pair_list: int32 [32, 2, 25], P(('groups', 'rows', 'tiles', 'sub')), parts along dimension 0, may hold values from -1 to 19, as said below
Outputs:
- solution: float32 [20480, 128], P(('groups', 'rows', 'tiles', 'sub')), parts along dimension 0
- residual: float32 [20480, 128], P(('groups', 'rows', 'tiles', 'sub')), parts along dimension 0
There are 2 independent parts, one for each index of `groups`. A program takes and returns all parts, laid end to end along the dimension named above; each array names one. Nothing has to cross between parts.
Inputs may be any that keep to these rules, and one draw needn't show every extreme that they name: Holder h lies in row group h // 4. Slot k of holder h is the pair i = pair_list[h, 0, k], j = pair_list[h, 1, k] with i in that row group and i <= j <= i + 4, j < 20. A holder's live pairs come first and the remaining slots hold -1 in both rows. Every pair appears at most once over all holders, and every diagonal pair (i, i) appears.
All inputs are finite; a program needn't handle non-finite values.
Results may differ from a plain program's by a relative error of at most 0.0024.
Values may be sent and summed in bfloat16 or wider, within the bound.
A program may use at most 64 MiB of HBM per device.

v0:
```python
import functools

import jax
import jax.numpy as jnp
from jax import lax
from jax.experimental import pallas as pl
from jax.experimental.pallas import tpu as pltpu
from jax.sharding import PartitionSpec as P

BLOCK = 512
HALF = 256
HROWS = 272
REACH = 4
SLOTS = 13
f32 = jnp.float32
bf16 = jnp.bfloat16


def split(v):
    hi = lax.reduce_precision(v, 8, 7)
    return hi, v - hi


def pack_points(points):
    hi, rest = split(points)
    lo = lax.reduce_precision(rest, 8, 7)
    both = hi + lo
    sq = jnp.sum(both * both, axis=1)
    n1, rest = split(sq)
    n2, n3 = split(rest)
    blocks = points.shape[0] // BLOCK
    feats = jnp.concatenate([hi, lo], axis=1).astype(bf16).reshape(blocks, 2, HALF, 128)
    pieces = jnp.stack([n1, n2, n3], axis=0).reshape(3, blocks, 2, 2, 128)
    pieces = pieces.transpose(1, 2, 3, 0, 4).reshape(blocks, 2, 6, 128)
    pieces = jnp.pad(pieces, ((0, 0), (0, 0), (0, 10), (0, 0))).astype(bf16)
    return jnp.concatenate([feats, pieces], axis=2)


def kernel(nz, nx, cap, tgt, pts, pairs, sol, res, pbuf, d0, d1, kbuf, abuf, na, acc, r1, dir2,
           pres, prevp, red1, red2, loc, gs, gr, gf, pzs, pzr, pfs, pfr, dzs, dzr, dfs, dfr,
           prs, prr, qs, qr, r1s, r1r, r2s, r2r):
    T = nx * 2
    R = tgt.shape[0]
    U = BLOCK // T
    UPH = T // 2
    x = lax.axis_index("tiles")
    c = lax.axis_index("sub")
    z = lax.axis_index("rows")
    t = x * 2 + c
    b0 = (5 * t) // T
    b1 = (5 * t + 4) // T
    b0c = (10 * x) // T
    b1c = (10 * x + 9) // T
    has_prev = z > 0
    has_next = z < nz - 1

    def partner():
        return {"sub": 1 - c}

    def have(e):
        if e < 4:
            return jnp.logical_and(has_prev, e + 1 >= b0c + 1)
        return jnp.logical_and(has_next, e - 9 <= b1c - 1)

    def rcopy(src, dst, s, r, dev):
        return pltpu.make_async_remote_copy(
            src_ref=src, dst_ref=dst, send_sem=s, recv_sem=r, device_id=dev,
            device_id_type=pl.DeviceIdType.MESH)

    EXT = (3, 9, 2, 10, 1, 11, 0, 12)

    own_rows = pl.ds(pl.multiple_of(REACH * BLOCK + t * R, 64), R)
    lc = pltpu.make_async_copy(pts, pbuf.at[pl.ds(4, 5)], loc)
    lc.start()
    d0[own_rows, :] = tgt[...].astype(bf16)
    lane = lax.broadcasted_iota(jnp.int32, (1, 128), 1)
    mine = jnp.zeros((1, 128), f32)
    for k in range(cap):
        left = pairs[0, 0, k]
        right = pairs[0, 1, k]
        code = jnp.where(left >= 0, (left - z * 5) * 5 + right - left, -100)
        hit = jnp.logical_or(lane == code, lane == code + 25)
        mine = jnp.where(hit, 1.0, mine)
    pres[t] = jnp.broadcast_to(mine, (8, 128))

    bar = pltpu.get_barrier_semaphore()

    def mates():
        for o in range(1, T):
            ot = lax.rem(t + o, T)
            yield o, ot, {"tiles": ot // 2, "sub": lax.rem(ot, 2)}

    def ranks():
        for o in range(1, nz):
            oz = lax.rem(z + o, nz)
            yield o, oz, {"rows": oz}

    for _, _, dev in mates():
        pl.semaphore_signal(bar, inc=1, device_id=dev, device_id_type=pl.DeviceIdType.MESH)
    for _, _, dev in ranks():
        pl.semaphore_signal(bar, inc=1, device_id=dev, device_id_type=pl.DeviceIdType.MESH)
    pl.semaphore_wait(bar, T - 1 + nz - 1)

    def gather_copies(it, d):
        view = d.at[own_rows]
        out = [rcopy(view, view, gs.at[it, 0], gr.at[it, t], partner())]
        for o in range(1, nx):
            out.append(rcopy(view, view, gs.at[it, o], gr.at[it, t], {"tiles": lax.rem(x + o, nx)}))
        return out

    def gather_from(it, d, o):
        src_t = lax.rem(x + nx - o, nx) * 2 + c
        rows = pl.ds(pl.multiple_of(REACH * BLOCK + src_t * R, 64), R)
        return (rcopy(d.at[rows], d.at[rows], gs.at[it, o], gr.at[it, src_t], partner()),
                rcopy(d.at[rows], d.at[rows], gf.at[it, o], gr.at[it, src_t], partner()))

    def gather_forward(it, d):
        for o in range(1, nx):
            inn, fwd = gather_from(it, d, o)
            inn.wait_recv()
            fwd.start()

    def gather_wait(it, d):
        for xx in range(nx):
            src_t = xx * 2 + (1 - c)
            rows = pl.ds(pl.multiple_of(REACH * BLOCK + src_t * R, 64), R)
            rcopy(d.at[rows], d.at[rows], gs.at[it, 0], gr.at[it, src_t], partner()).wait_recv()

    def p_send(e):
        if e < 4:
            return rcopy(pts.at[e + 1, c], pbuf.at[e, c], pzs.at[e], pzr.at[e], {"rows": z + 1})
        return rcopy(pts.at[e - 9, c], pbuf.at[e, c], pzs.at[e], pzr.at[e], {"rows": z - 1})

    def can_send(e):
        if e < 4:
            return jnp.logical_and(has_next, e + 1 >= b0c + 1)
        return jnp.logical_and(has_prev, e - 9 <= b1c - 1)

    def p_fwd(e):
        return rcopy(pbuf.at[e, c], pbuf.at[e, c], pfs.at[e], pfr.at[e], partner())

    def half_rows(e, h):
        return pl.ds(pl.multiple_of(e * BLOCK + h * HALF, HALF), HALF)

    def d_send(it, d, e):
        s = e + 5 if e < 4 else e - 5
        dev = {"rows": z + 1} if e < 4 else {"rows": z - 1}
        return rcopy(d.at[half_rows(s, c)], d.at[half_rows(e, c)], dzs.at[it, e], dzr.at[it, e], dev)

    def d_fwd(it, d, e):
        v = d.at[half_rows(e, c)]
        return rcopy(v, v, dfs.at[it, e], dfr.at[it, e], partner())

    def d_fwd_in(it, d, e):
        v = d.at[half_rows(e, 1 - c)]
        return rcopy(v, v, dfs.at[it, e], dfr.at[it, e], partner())

    def pfwd_in(e):
        v = pbuf.at[e, 1 - c]
        return rcopy(v, v, pfs.at[e], pfr.at[e], partner())

    def each(cond, fn):
        for e in EXT:
            @pl.when(cond(e))
            def _(e=e):
                fn(e)

    pc = [rcopy(pres.at[t], pres.at[t], prs.at[o], prr.at[t], dev) for o, _, dev in mates()]
    for cp in pc:
        cp.start()
    for cp in gather_copies(0, d0):
        cp.start()
    each(can_send, lambda e: p_send(e).start())
    lc.wait()

    for k in range(5):
        g = 5 * t + k
        hb = g // UPH
        off = pl.multiple_of(lax.rem(g, UPH) * U, U)
        rows = pbuf[4 + hb // 2, lax.rem(hb, 2), pl.ds(off, U), :].astype(f32)
        turned = pltpu.roll(rows, 64, 1)
        abuf[k * U:(k + 1) * U, 0:128] = (-2.0 * rows).astype(bf16)
        abuf[k * U:(k + 1) * U, 128:256] = (-2.0 * turned).astype(bf16)
        na[k * U:(k + 1) * U, :] = jnp.broadcast_to(
            jnp.sum(rows * (rows + turned), axis=1, keepdims=True), (U, 128))

    for o, ot, dev in mates():
        rcopy(pres.at[ot], pres.at[ot], prs.at[o], prr.at[ot], dev).wait_recv()
    own = pres[0]
    for i in range(1, T):
        own = own + pres[i]
    prevp[1] = jnp.where(lane >= 25, own, 0.0)
    prevp[2] = jnp.where(lane < 25, own, 0.0)

    def q_copy():
        return rcopy(prevp.at[2], prevp.at[0], qs, qr, {"rows": z + 1})

    @pl.when(has_next)
    def _():
        q_copy().start()

    @pl.when(jnp.logical_not(has_prev))
    def _():
        prevp[0] = jnp.zeros((8, 128), f32)

    def build(e, listed):
        for h in range(2):
            blk = pbuf[e, h]
            b = blk[:HALF]
            nr = blk[HALF:].astype(f32)
            nc = jnp.concatenate([nr[0:1] + nr[1:2] + nr[2:3], nr[3:4] + nr[4:5] + nr[5:6]], axis=1)
            gram = lax.dot_general(abuf[...], jnp.concatenate([b, b], axis=1),
                                   (((1,), (1,)), ((), ())), preferred_element_type=f32)
            for k in range(5):
                i = (5 * t + k) // T
                j = e - 4
                dist = jnp.abs(i - j)
                code = jnp.where(dist <= REACH, (jnp.minimum(i, j) + 5) * 5 + dist, 127)
                m = jnp.sum(jnp.where(lane == code, listed, 0.0), axis=1, keepdims=True)
                u = slice(k * U, (k + 1) * U)
                s = gram[u] + nc + na[u, 0:1]
                s = jnp.maximum(s, 1e-20)
                r = s * lax.rsqrt(s) * (1.0 / 12.0)
                base = jnp.maximum(m - r, 0.0)
                base2 = base * base
                kt = base2 * base2 * (4.0 * r + 1.0)
                kbuf[e - b0, u, h * HALF:(h + 1) * HALF] = kt.astype(bf16)

    def builds(lo, hi, listed):
        def body(e, carry):
            build(e, listed)
            return carry
        lax.fori_loop(lo, hi, body, 0)

    def mults(d, lo, hi):
        def body(e, carry):
            acc[...] += jnp.dot(kbuf[e - b0], d[pl.ds(pl.multiple_of(e * BLOCK, BLOCK), BLOCK), :],
                                preferred_element_type=f32)
            return carry
        lax.fori_loop(lo, hi, body, 0)

    prev_lo = jnp.where(has_prev, b0, 4)
    next_hi = jnp.where(has_next, b1 + 9, 9)

    own_list = jnp.minimum(prevp[1, 0:1], 1.0)
    acc[...] = jnp.zeros_like(acc)
    builds(4, 6, own_list)
    gather_forward(0, d0)
    builds(6, 7, own_list)
    gather_wait(0, d0)
    each(can_send, lambda e: d_send(0, d0, e).start())
    builds(7, 9, own_list)

    def p_take(e):
        p_send(e).wait_recv()
        p_fwd(e).start()

    each(have, p_take)
    mults(d0, 4, 9)

    @pl.when(has_prev)
    def _():
        q_copy().wait_recv()
    each(have, lambda e: pfwd_in(e).wait_recv())
    whole_list = jnp.minimum(prevp[1, 0:1] + prevp[0, 0:1], 1.0)
    builds(prev_lo, 4, whole_list)
    builds(9, next_hi, whole_list)

    def d_finish(it, d):
        def take(e):
            d_send(it, d, e).wait_recv()
            d_fwd(it, d, e).start()
        each(have, take)
        each(have, lambda e: d_fwd_in(it, d, e).wait_recv())
        mults(d, prev_lo, 4)
        mults(d, 9, next_hi)

    d_finish(0, d0)

    def total(it, sums):
        rows = [*sums] + [jnp.zeros((8 - len(sums), 128), f32)]
        red1[it, t] = jnp.concatenate(rows, axis=0)
        v = red1.at[it, t]
        for o, ot, dev in mates():
            rcopy(v, v, r1s.at[it, o], r1r.at[it, t], dev).start()
        for o, ot, dev in mates():
            w = red1.at[it, ot]
            rcopy(w, w, r1s.at[it, o], r1r.at[it, ot], dev).wait_recv()
        a = red1[it, 0]
        for i in range(1, T):
            a = a + red1[it, i]
        red2[it, z] = a
        v = red2.at[it, z]
        for o, oz, dev in ranks():
            rcopy(v, v, r2s.at[it, o], r2r.at[it, z], dev).start()
        for o, oz, dev in ranks():
            w = red2.at[it, oz]
            rcopy(w, w, r2s.at[it, o], r2r.at[it, oz], dev).wait_recv()
        a = red2[it, 0]
        for i in range(1, nz):
            a = a + red2[it, i]
        return a

    def colsum(v):
        return jnp.sum(v, axis=0, keepdims=True)

    tv = tgt[...]
    q = 0.25 * tv + acc[...] * (1.0 / BLOCK)
    sums = total(0, (colsum(tv * tv), colsum(tv * q), colsum(q * q)))
    rr, tq, qq = sums[0:1], sums[1:2], sums[2:3]
    alpha = rr / tq
    beta = (alpha * alpha * qq - rr) / rr
    q = 0.25 * tgt[...] + acc[...] * (1.0 / BLOCK)
    first = tgt[...] - alpha * q
    r1[...] = first
    second = first + beta * tgt[...]
    dir2[...] = second
    d1[own_rows, :] = second.astype(bf16)
    for cp in gather_copies(1, d1):
        cp.start()
    acc[...] = jnp.zeros_like(acc)
    gather_forward(1, d1)
    gather_wait(1, d1)
    each(can_send, lambda e: d_send(1, d1, e).start())
    mults(d1, 4, 9)
    d_finish(1, d1)
    q = 0.25 * dir2[...] + acc[...] * (1.0 / BLOCK)
    sums = total(1, (colsum(r1[...] * r1[...]), colsum(dir2[...] * q)))
    alpha2 = sums[0:1] / sums[1:2]
    q = 0.25 * dir2[...] + acc[...] * (1.0 / BLOCK)
    sol[...] = alpha * tgt[...] + alpha2 * dir2[...]
    res[...] = r1[...] - alpha2 * q

    for cp in pc:
        cp.wait_send()

    @pl.when(has_next)
    def _():
        q_copy().wait_send()
    each(can_send, lambda e: p_send(e).wait_send())
    each(have, lambda e: p_fwd(e).wait_send())
    for it, d in enumerate((d0, d1)):
        for cp in gather_copies(it, d):
            cp.wait_send()
        for o in range(1, nx):
            gather_from(it, d, o)[1].wait_send()
        each(can_send, lambda e: d_send(it, d, e).wait_send())
        each(have, lambda e: d_fwd(it, d, e).wait_send())
        for o, ot, dev in mates():
            rcopy(red1.at[it, t], red1.at[it, t], r1s.at[it, o], r1r.at[it, t], dev).wait_send()
        for o, oz, dev in ranks():
            rcopy(red2.at[it, z], red2.at[it, z], r2s.at[it, o], r2r.at[it, z], dev).wait_send()


def local(nz, nx, points, targets, pair_list):
    T = nx * 2
    R = targets.shape[0]
    pts = pack_points(points)
    dma = pltpu.SemaphoreType.DMA
    vmem = pl.BlockSpec(memory_space=pltpu.VMEM)
    shape = jax.ShapeDtypeStruct(targets.shape, f32)
    return pl.pallas_call(
        functools.partial(kernel, nz, nx, pair_list.shape[2]),
        out_shape=(shape, shape),
        in_specs=[vmem, pl.BlockSpec(memory_space=pl.ANY), pl.BlockSpec(memory_space=pltpu.SMEM)],
        out_specs=(vmem, vmem),
        scratch_shapes=[
            pltpu.VMEM((SLOTS, 2, HROWS, 128), bf16),
            pltpu.VMEM((SLOTS * BLOCK, 128), bf16),
            pltpu.VMEM((SLOTS * BLOCK, 128), bf16),
            pltpu.VMEM((10, R, BLOCK), bf16),
            pltpu.VMEM((R, 256), bf16),
            pltpu.VMEM((R, 128), f32),
            pltpu.VMEM((R, 128), f32),
            pltpu.VMEM((R, 128), f32),
            pltpu.VMEM((R, 128), f32),
            pltpu.VMEM((T, 8, 128), f32),
            pltpu.VMEM((3, 8, 128), f32),
            pltpu.VMEM((2, T, 8, 128), f32),
            pltpu.VMEM((2, nz, 8, 128), f32),
            dma,
            dma((2, nx)), dma((2, T)), dma((2, nx)),
            dma((SLOTS,)), dma((SLOTS,)), dma((SLOTS,)), dma((SLOTS,)),
            dma((2, SLOTS)), dma((2, SLOTS)), dma((2, SLOTS)), dma((2, SLOTS)),
            dma((T,)), dma((T,)), dma, dma,
            dma((2, T)), dma((2, T)), dma((2, nz)), dma((2, nz)),
        ],
        compiler_params=pltpu.CompilerParams(
            collective_id=0, has_side_effects=True, vmem_limit_bytes=48 * 1024 * 1024),
        cost_estimate=pl.CostEstimate(flops=5 * 10**9, bytes_accessed=2 * 10**6, transcendentals=3 * 10**6),
    )(targets, pts, pair_list)


def solution(mesh):
    nz, nx = mesh.shape["rows"], mesh.shape["tiles"]
    in_specs = (
        P(("groups", "rows"), None),
        P(("groups", "rows", "tiles", "sub"), None),
        P(("groups", "rows", "tiles", "sub"), None, None),
    )
    out_specs = (
        P(("groups", "rows", "tiles", "sub"), None),
        P(("groups", "rows", "tiles", "sub"), None),
    )
    return jax.shard_map(functools.partial(local, nz, nx), mesh=mesh, in_specs=in_specs,
                         out_specs=out_specs, check_vma=False)
```

profile of v0, /device:TPU:0, one launch (start us, length us, event | category | flops | bytes accessed | tf_op | source)
XLA Modules:
  0.0 56.7 jit_solution(14104485726326626496)
XLA Ops:
  0.6 1.3 %reduce-precision_convert_fusion = (bf16[2560,64]{0,1:T(8,128)(2,1)S(1)}, f32[2560]{0:T(1024)S(1)}, bf16[2560,64]{0,1:T(8,128)(2,1)S(1)}) fusion(f32[2560,64]{0,1:T(8,128)} %param.3), kind=kLoop, calls=%fused_computation.4 | loop fusion | flops 1308160 | bytes 1320960 | tf_op jit(solution)/shard_map/convert.10
  2.0 0.3 copy.10
  2.3 0.3 copy.11
  2.7 0.0 copy-start
  2.7 0.0 copy-start.1
  2.7 0.4 fusion.1.pts
  3.1 0.6 %copy-done = f32[640,128]{1,0:T(8,128)S(1)} copy-done((f32[640,128]{1,0:T(8,128)S(1)}, f32[640,128]{1,0:T(8,128)}, u32[]{:S(2)}) %copy-start) | copy-done | bytes 327704
  3.6 0.0 copy-done.1
  3.6 51.6 %shard_map.50 = (f32[640,128]{1,0:T(8,128)S(1)}, f32[640,128]{1,0:T(8,128)S(1)}) custom-call(f32[640,128]{1,0:T(8,128)S(1)} %copy-done, bf16[5,2,272,128]{3,2,1,0:T(8,128)(2,1)S(1)} %fusion.1.pts, s32[1,2,25]{2,1,0:T(2,128)S(1)} %copy-done.1), custom_call_target="tpu_custom_call" | custom-call | flops 5000000000 | bytes 2000000 | tf_op jit(solution)/shard_map/pallas_call | solution.py:362
  55.2 0.7 %copy.16 = f32[640,128]{1,0:T(8,128)} copy(f32[640,128]{1,0:T(8,128)S(1)} %get-tuple-element.10) | data formatting | bytes 655360
  56.0 0.7 %copy.17 = f32[640,128]{1,0:T(8,128)} copy(f32[640,128]{1,0:T(8,128)S(1)} %get-tuple-element.11) | data formatting | bytes 655360
  (5 shorter events, 0.1 us)
Async XLA Ops:
  2.7 1.0 %copy-start = (f32[640,128]{1,0:T(8,128)S(1)}, f32[640,128]{1,0:T(8,128)}, u32[]{:S(2)}) copy-start(f32[640,128]{1,0:T(8,128)} %tgt.1) | copy-start | bytes 983044
  2.7 1.0 %copy-start.1 = (s32[1,2,25]{2,1,0:T(2,128)S(1)}, s32[1,2,25]{2,1,0:T(2,128)}, u32[]{:S(2)}) copy-start(s32[1,2,25]{2,1,0:T(2,128)} %pairs.1) | copy-start | bytes 604
where the time goes:
time: 56.9 us; the launch traced here: 56.7 us
  Pallas kernels  51.6 us (91%)
  local copies, waits for them, and re-layouts  2.72 us (5%)
  other arithmetic  1.68 us (3%)
  between operations  0.71 us (1%)
    pallas_call x1, Pallas kernels, local(): pl.pallas_call(functools.partial(kernel, nz, nx, pair_list.shape[2]), out...  51.6 us
    unnamed x6, local copies, waits for them, and re-layouts  2.04 us
    another operation x2, other arithmetic  1.28 us

commit v1 on v0

--- a/solution.py
+++ b/solution.py
@@ -95,11 +95,18 @@
             oz = lax.rem(z + o, nz)
             yield o, oz, {"rows": oz}
 
-    for _, _, dev in mates():
+    flat = T * nz <= 16
+    me = z * T + t
+
+    def others():
+        for o in range(1, T * nz):
+            m = lax.rem(me + o, T * nz)
+            yield o, m, {"rows": m // T, "tiles": lax.rem(m, T) // 2, "sub": lax.rem(m, 2)}
+
+    greeted = list(others()) if flat else [*mates(), *ranks()]
+    for _, _, dev in greeted:
         pl.semaphore_signal(bar, inc=1, device_id=dev, device_id_type=pl.DeviceIdType.MESH)
-    for _, _, dev in ranks():
-        pl.semaphore_signal(bar, inc=1, device_id=dev, device_id_type=pl.DeviceIdType.MESH)
-    pl.semaphore_wait(bar, T - 1 + nz - 1)
+    pl.semaphore_wait(bar, len(greeted))
 
     def gather_copies(it, d):
         view = d.at[own_rows]
@@ -119,6 +126,7 @@
             inn, fwd = gather_from(it, d, o)
             inn.wait_recv()
             fwd.start()
+            d_start(it, d, o)
 
     def gather_wait(it, d):
         for xx in range(nx):
@@ -139,21 +147,31 @@
     def p_fwd(e):
         return rcopy(pbuf.at[e, c], pbuf.at[e, c], pfs.at[e], pfr.at[e], partner())
 
-    def half_rows(e, h):
-        return pl.ds(pl.multiple_of(e * BLOCK + h * HALF, HALF), HALF)
-
-    def d_send(it, d, e):
-        s = e + 5 if e < 4 else e - 5
-        dev = {"rows": z + 1} if e < 4 else {"rows": z - 1}
-        return rcopy(d.at[half_rows(s, c)], d.at[half_rows(e, c)], dzs.at[it, e], dzr.at[it, e], dev)
-
-    def d_fwd(it, d, e):
-        v = d.at[half_rows(e, c)]
-        return rcopy(v, v, dfs.at[it, e], dfr.at[it, e], partner())
-
-    def d_fwd_in(it, d, e):
-        v = d.at[half_rows(e, 1 - c)]
-        return rcopy(v, v, dfs.at[it, e], dfr.at[it, e], partner())
+    def d_unit(it, d, way, o, k, cc):
+        g = 5 * (lax.rem(x + nx - o, nx) * 2 + cc) + k
+        b = g // T
+        needed = b >= b0c + 1 if way == 0 else b <= b1c - 1
+        shift = -BLOCK if way == 0 else (REACH + 5) * BLOCK
+        n = (way * nx + o) * 5 + k
+        src = d.at[pl.ds(pl.multiple_of(g * U + REACH * BLOCK, 64), U)]
+        dst = d.at[pl.ds(pl.multiple_of(jnp.where(needed, g * U + shift, 0), 64), U)]
+        dev = {"rows": z + 1 if way == 0 else z - 1}
+        can = jnp.logical_and(needed, has_next if way == 0 else has_prev)
+        got = jnp.logical_and(needed, has_prev if way == 0 else has_next)
+        return (can, got, lambda: rcopy(src, dst, dzs.at[it, n], dzr.at[it, n], dev),
+                lambda: rcopy(dst, dst, dfs.at[it, n], dfr.at[it, n], partner()))
+
+    def units(it, d, o, cc, which, fn):
+        for k in range(5):
+            for way in range(2):
+                can, got, sent, passed = d_unit(it, d, way, o, k, cc)
+
+                @pl.when(can if which == "can" else got)
+                def _():
+                    fn(sent, passed)
+
+    def d_start(it, d, o):
+        units(it, d, o, c, "can", lambda sent, passed: sent().start())
 
     def pfwd_in(e):
         v = pbuf.at[e, 1 - c]
@@ -170,6 +188,7 @@
         cp.start()
     for cp in gather_copies(0, d0):
         cp.start()
+    d_start(0, d0, 0)
     each(can_send, lambda e: p_send(e).start())
     lc.wait()
 
@@ -248,7 +267,6 @@
     gather_forward(0, d0)
     builds(6, 7, own_list)
     gather_wait(0, d0)
-    each(can_send, lambda e: d_send(0, d0, e).start())
     builds(7, 9, own_list)
 
     def p_take(e):
@@ -267,11 +285,13 @@
     builds(9, next_hi, whole_list)
 
     def d_finish(it, d):
-        def take(e):
-            d_send(it, d, e).wait_recv()
-            d_fwd(it, d, e).start()
-        each(have, take)
-        each(have, lambda e: d_fwd_in(it, d, e).wait_recv())
+        def take(sent, passed):
+            sent().wait_recv()
+            passed().start()
+        for o in range(nx):
+            units(it, d, o, c, "got", take)
+        for o in range(nx):
+            units(it, d, o, 1 - c, "got", lambda sent, passed: passed().wait_recv())
         mults(d, prev_lo, 4)
         mults(d, 9, next_hi)
 
@@ -279,6 +299,18 @@
 
     def total(it, sums):
         rows = [*sums] + [jnp.zeros((8 - len(sums), 128), f32)]
+        if flat:
+            red1[it, me] = jnp.concatenate(rows, axis=0)
+            v = red1.at[it, me]
+            for o, m, dev in others():
+                rcopy(v, v, r1s.at[it, o], r1r.at[it, me], dev).start()
+            for o, m, dev in others():
+                w = red1.at[it, m]
+                rcopy(w, w, r1s.at[it, o], r1r.at[it, m], dev).wait_recv()
+            a = red1[it, 0]
+            for i in range(1, T * nz):
+                a = a + red1[it, i]
+            return a
         red1[it, t] = jnp.concatenate(rows, axis=0)
         v = red1.at[it, t]
         for o, ot, dev in mates():
@@ -318,10 +350,10 @@
     d1[own_rows, :] = second.astype(bf16)
     for cp in gather_copies(1, d1):
         cp.start()
+    d_start(1, d1, 0)
     acc[...] = jnp.zeros_like(acc)
     gather_forward(1, d1)
     gather_wait(1, d1)
-    each(can_send, lambda e: d_send(1, d1, e).start())
     mults(d1, 4, 9)
     d_finish(1, d1)
     q = 0.25 * dir2[...] + acc[...] * (1.0 / BLOCK)
@@ -344,8 +376,13 @@
             cp.wait_send()
         for o in range(1, nx):
             gather_from(it, d, o)[1].wait_send()
-        each(can_send, lambda e: d_send(it, d, e).wait_send())
-        each(have, lambda e: d_fwd(it, d, e).wait_send())
+        for o in range(nx):
+            units(it, d, o, c, "can", lambda sent, passed: sent().wait_send())
+            units(it, d, o, c, "got", lambda sent, passed: passed().wait_send())
+        if flat:
+            for o, m, dev in others():
+                rcopy(red1.at[it, me], red1.at[it, me], r1s.at[it, o], r1r.at[it, me], dev).wait_send()
+            continue
         for o, ot, dev in mates():
             rcopy(red1.at[it, t], red1.at[it, t], r1s.at[it, o], r1r.at[it, t], dev).wait_send()
         for o, oz, dev in ranks():
@@ -354,6 +391,7 @@
 
 def local(nz, nx, points, targets, pair_list):
     T = nx * 2
+    n_red = T * nz if T * nz <= 16 else T
     R = targets.shape[0]
     pts = pack_points(points)
     dma = pltpu.SemaphoreType.DMA
@@ -376,14 +414,14 @@
             pltpu.VMEM((R, 128), f32),
             pltpu.VMEM((T, 8, 128), f32),
             pltpu.VMEM((3, 8, 128), f32),
-            pltpu.VMEM((2, T, 8, 128), f32),
+            pltpu.VMEM((2, n_red, 8, 128), f32),
             pltpu.VMEM((2, nz, 8, 128), f32),
             dma,
             dma((2, nx)), dma((2, T)), dma((2, nx)),
             dma((SLOTS,)), dma((SLOTS,)), dma((SLOTS,)), dma((SLOTS,)),
-            dma((2, SLOTS)), dma((2, SLOTS)), dma((2, SLOTS)), dma((2, SLOTS)),
+            dma((2, 10 * nx)), dma((2, 10 * nx)), dma((2, 10 * nx)), dma((2, 10 * nx)),
             dma((T,)), dma((T,)), dma, dma,
-            dma((2, T)), dma((2, T)), dma((2, nz)), dma((2, nz)),
+            dma((2, n_red)), dma((2, n_red)), dma((2, nz)), dma((2, nz)),
         ],
         compiler_params=pltpu.CompilerParams(
             collective_id=0, has_side_effects=True, vmem_limit_bytes=48 * 1024 * 1024),

time: 56.9 us -> 55.3 us (0.972)
  Pallas kernels: 51.6 us -> 50 us
    pallas_call x1, Pallas kernels: 51.6 us -> 50 us  [local(): pl.pallas_call(functools.partial(kernel, nz, nx, pair_list.shape[2]), out...]
where the time goes in v1:
time: 55.3 us; the launch traced here: 55.1 us
  Pallas kernels  50 us (90%)
  local copies, waits for them, and re-layouts  2.72 us (5%)
  other arithmetic  1.68 us (3%)
  between operations  0.71 us (1%)
    pallas_call x1, Pallas kernels, local(): pl.pallas_call(functools.partial(kernel, nz, nx, pair_list.shape[2]), out...  50 us
    unnamed x6, local copies, waits for them, and re-layouts  2.04 us
    another operation x2, other arithmetic  1.28 us

profile of v1, /device:TPU:0, one launch (start us, length us, event | category | flops | bytes accessed | tf_op | source)
XLA Modules:
  0.0 55.1 jit_solution(15672954821249129825)
XLA Ops:
  0.6 1.3 %reduce-precision_convert_fusion = (bf16[2560,64]{0,1:T(8,128)(2,1)S(1)}, f32[2560]{0:T(1024)S(1)}, bf16[2560,64]{0,1:T(8,128)(2,1)S(1)}) fusion(f32[2560,64]{0,1:T(8,128)} %param.3), kind=kLoop, calls=%fused_computation.4 | loop fusion | flops 1308160 | bytes 1320960 | tf_op jit(solution)/shard_map/convert.10
  2.0 0.3 copy.10
  2.3 0.3 copy.11
  2.7 0.0 copy-start
  2.7 0.0 copy-start.1
  2.7 0.4 fusion.1.pts
  3.1 0.6 %copy-done = f32[640,128]{1,0:T(8,128)S(1)} copy-done((f32[640,128]{1,0:T(8,128)S(1)}, f32[640,128]{1,0:T(8,128)}, u32[]{:S(2)}) %copy-start) | copy-done | bytes 327704
  3.6 0.0 copy-done.1
  3.6 50.0 %shard_map.50 = (f32[640,128]{1,0:T(8,128)S(1)}, f32[640,128]{1,0:T(8,128)S(1)}) custom-call(f32[640,128]{1,0:T(8,128)S(1)} %copy-done, bf16[5,2,272,128]{3,2,1,0:T(8,128)(2,1)S(1)} %fusion.1.pts, s32[1,2,25]{2,1,0:T(2,128)S(1)} %copy-done.1), custom_call_target="tpu_custom_call" | custom-call | flops 5000000000 | bytes 2000000 | tf_op jit(solution)/shard_map/pallas_call | solution.py:400
  53.6 0.7 %copy.16 = f32[640,128]{1,0:T(8,128)} copy(f32[640,128]{1,0:T(8,128)S(1)} %get-tuple-element.10) | data formatting | bytes 655360
  54.4 0.7 %copy.17 = f32[640,128]{1,0:T(8,128)} copy(f32[640,128]{1,0:T(8,128)S(1)} %get-tuple-element.11) | data formatting | bytes 655360
  (5 shorter events, 0.1 us)
Async XLA Ops:
  2.7 1.0 %copy-start = (f32[640,128]{1,0:T(8,128)S(1)}, f32[640,128]{1,0:T(8,128)}, u32[]{:S(2)}) copy-start(f32[640,128]{1,0:T(8,128)} %tgt.1) | copy-start | bytes 983044
  2.7 1.0 %copy-start.1 = (s32[1,2,25]{2,1,0:T(2,128)S(1)}, s32[1,2,25]{2,1,0:T(2,128)}, u32[]{:S(2)}) copy-start(s32[1,2,25]{2,1,0:T(2,128)} %pairs.1) | copy-start | bytes 604

commit v2 on v1

--- a/solution.py
+++ b/solution.py
@@ -69,6 +69,30 @@
 
     EXT = (3, 9, 2, 10, 1, 11, 0, 12)
 
+    bar = pltpu.get_barrier_semaphore()
+
+    def mates():
+        for o in range(1, T):
+            ot = lax.rem(t + o, T)
+            yield o, ot, {"tiles": ot // 2, "sub": lax.rem(ot, 2)}
+
+    def ranks():
+        for o in range(1, nz):
+            oz = lax.rem(z + o, nz)
+            yield o, oz, {"rows": oz}
+
+    flat = T * nz <= 16
+    me = z * T + t
+
+    def others():
+        for o in range(1, T * nz):
+            m = lax.rem(me + o, T * nz)
+            yield o, m, {"rows": m // T, "tiles": lax.rem(m, T) // 2, "sub": lax.rem(m, 2)}
+
+    greeted = list(others()) if flat else [*mates(), *ranks()]
+    for _, _, dev in greeted:
+        pl.semaphore_signal(bar, inc=1, device_id=dev, device_id_type=pl.DeviceIdType.MESH)
+
     own_rows = pl.ds(pl.multiple_of(REACH * BLOCK + t * R, 64), R)
     lc = pltpu.make_async_copy(pts, pbuf.at[pl.ds(4, 5)], loc)
     lc.start()
@@ -83,29 +107,6 @@
         mine = jnp.where(hit, 1.0, mine)
     pres[t] = jnp.broadcast_to(mine, (8, 128))
 
-    bar = pltpu.get_barrier_semaphore()
-
-    def mates():
-        for o in range(1, T):
-            ot = lax.rem(t + o, T)
-            yield o, ot, {"tiles": ot // 2, "sub": lax.rem(ot, 2)}
-
-    def ranks():
-        for o in range(1, nz):
-            oz = lax.rem(z + o, nz)
-            yield o, oz, {"rows": oz}
-
-    flat = T * nz <= 16
-    me = z * T + t
-
-    def others():
-        for o in range(1, T * nz):
-            m = lax.rem(me + o, T * nz)
-            yield o, m, {"rows": m // T, "tiles": lax.rem(m, T) // 2, "sub": lax.rem(m, 2)}
-
-    greeted = list(others()) if flat else [*mates(), *ranks()]
-    for _, _, dev in greeted:
-        pl.semaphore_signal(bar, inc=1, device_id=dev, device_id_type=pl.DeviceIdType.MESH)
     pl.semaphore_wait(bar, len(greeted))
 
     def gather_copies(it, d):

time: 55.3 us -> 55 us (level)
  no operation moved by 1% of the time
where the time goes in v2:
time: 55 us; the launch traced here: 54.8 us
  Pallas kernels  49.7 us (90%)
  local copies, waits for them, and re-layouts  2.72 us (5%)
  other arithmetic  1.68 us (3%)
  between operations  0.71 us (1%)
    pallas_call x1, Pallas kernels, local(): pl.pallas_call(functools.partial(kernel, nz, nx, pair_list.shape[2]), out...  49.7 us
    unnamed x6, local copies, waits for them, and re-layouts  2.04 us
    another operation x2, other arithmetic  1.28 us

profile of v2, /device:TPU:0, one launch (start us, length us, event | category | flops | bytes accessed | tf_op | source)
XLA Modules:
  0.0 54.8 jit_solution(6902033743495274597)
XLA Ops:
  0.6 1.3 %reduce-precision_convert_fusion = (bf16[2560,64]{0,1:T(8,128)(2,1)S(1)}, f32[2560]{0:T(1024)S(1)}, bf16[2560,64]{0,1:T(8,128)(2,1)S(1)}) fusion(f32[2560,64]{0,1:T(8,128)} %param.3), kind=kLoop, calls=%fused_computation.4 | loop fusion | flops 1308160 | bytes 1320960 | tf_op jit(solution)/shard_map/convert.10
  2.0 0.3 copy.10
  2.3 0.3 copy.11
  2.7 0.0 copy-start
  2.7 0.0 copy-start.1
  2.7 0.4 fusion.1.pts
  3.1 0.6 %copy-done = f32[640,128]{1,0:T(8,128)S(1)} copy-done((f32[640,128]{1,0:T(8,128)S(1)}, f32[640,128]{1,0:T(8,128)}, u32[]{:S(2)}) %copy-start) | copy-done | bytes 327704
  3.6 0.0 copy-done.1
  3.6 49.7 %shard_map.50 = (f32[640,128]{1,0:T(8,128)S(1)}, f32[640,128]{1,0:T(8,128)S(1)}) custom-call(f32[640,128]{1,0:T(8,128)S(1)} %copy-done, bf16[5,2,272,128]{3,2,1,0:T(8,128)(2,1)S(1)} %fusion.1.pts, s32[1,2,25]{2,1,0:T(2,128)S(1)} %copy-done.1), custom_call_target="tpu_custom_call" | custom-call | flops 5000000000 | bytes 2000000 | tf_op jit(solution)/shard_map/pallas_call | solution.py:401
  53.3 0.7 %copy.16 = f32[640,128]{1,0:T(8,128)} copy(f32[640,128]{1,0:T(8,128)S(1)} %get-tuple-element.10) | data formatting | bytes 655360
  54.0 0.7 %copy.17 = f32[640,128]{1,0:T(8,128)} copy(f32[640,128]{1,0:T(8,128)S(1)} %get-tuple-element.11) | data formatting | bytes 655360
  (5 shorter events, 0.1 us)
Async XLA Ops:
  2.7 1.0 %copy-start = (f32[640,128]{1,0:T(8,128)S(1)}, f32[640,128]{1,0:T(8,128)}, u32[]{:S(2)}) copy-start(f32[640,128]{1,0:T(8,128)} %tgt.1) | copy-start | bytes 983044
  2.7 1.0 %copy-start.1 = (s32[1,2,25]{2,1,0:T(2,128)S(1)}, s32[1,2,25]{2,1,0:T(2,128)}, u32[]{:S(2)}) copy-start(s32[1,2,25]{2,1,0:T(2,128)} %pairs.1) | copy-start | bytes 604
